TPU v7x, 32 devices: a whole 2x2x4 slice. The times are simulated.
32 devices in a mesh: plane: 8 (over z, x), strip: 4 (over y, core).
Axes of the slice: x: 2, y: 2, z: 4, core: 2. Of those that a mesh axis runs over, the one named last changes fastest.
Arguments:
- current: float32 [8, 256, 3072], P('plane', 'strip'), may hold values from -60 to 60, as said below
- cond_x: bfloat16 [8, 256, 3072], P('plane', 'strip'), may hold values from 0.5 to 5
- cond_y: bfloat16 [8, 256, 3072], P('plane', 'strip'), may hold values from 0.5 to 5
- tile_class: int32 [8, 16, 24], P('plane', 'strip'), may hold values from 0 to 7
- class_diag: float32 [8], replicated, may hold values from 0.2 to 2
- via_count: int32 [8, 16, 24], P('plane', 'strip'), may hold values from 0 to 3, as said below
Outputs:
- voltage: float32 [8, 256, 3072], P('plane', 'strip')
- residual_ratio: float32 [4, 8], P(None, 'plane')
Inputs may be any that keep to these rules, and one draw needn't show every extreme that they name: `current`: load currents; any value in the range. `via_count`: in the rows of one device of each plane exactly 24 tiles have a nonzero count; planes 2k and 2k + 1 have equal counts everywhere.
All inputs are finite; a program needn't handle non-finite values.
Results may differ from a plain program's by a relative error of at most 0.0003.
Values sent between devices are 32-bit elements; how exact they have to be, the bound alone decides.
A program may use at most 64 MiB of HBM per device.

v0:
```python
import jax
import jax.numpy as jnp
from jax import lax
from jax.sharding import PartitionSpec as P

TILE_ROWS = 16
TILE_COLS = 128
CLASSES = 8
SWEEPS = 4


ground_cond = 0.5
via_cond = 3.0
bound_low = 0.05
bound_high = 2.0


def swapped(block, axis, distance):
    count = lax.axis_size(axis)
    route = []
    for low in range(count):
        high = low | 1 << distance
        if high != low and high < count:
            route += [(low, high), (high, low)]
    return lax.ppermute(block, axis, route)


def shifted(shard, axis, by):
    size = lax.axis_size(axis)
    pairs = [(i, i + by) for i in range(size) if 0 <= i + by < size]
    return lax.ppermute(shard, axis, pairs)


def padded_2(shard, sides, width):
    for axis, dim in sides:
        size, length = (lax.axis_size(axis), shard.shape[dim])
        up = [(i, (i + 1) % size) for i in range(size - 1)]
        down = [(j, i) for i, j in up]
        last = lax.slice_in_dim(shard, length - width, length, axis=dim)
        initial = lax.slice_in_dim(shard, 0, width, axis=dim)
        before = lax.ppermute(last, axis, up)
        after = lax.ppermute(initial, axis, down)
        shard = jnp.concatenate([before, shard, after], axis=dim)
    return shard


def cheby_coeffs(sweeps):
    theta = (bound_high + bound_low) / 2.0
    delta = (bound_high - bound_low) / 2.0
    sigma = theta / delta
    rho = 1.0 / sigma
    coeffs = []
    for step in range(sweeps - 1):
        rho_new = 1.0 / (2.0 * sigma - rho)
        coeffs.append((rho_new * rho, 2.0 * rho_new / delta))
        rho = rho_new
    return (theta, coeffs)


def expand(tiles):
    return jnp.repeat(jnp.repeat(tiles, TILE_ROWS, axis=0), TILE_COLS, axis=1)


def shift_cols(field):
    return jnp.pad(field, ((0, 0), (1, 0)))[:, :-1]


def partner_of(field):
    return swapped(field, "plane", 0)


def on_device(current, cond_x, cond_y, tile_class, class_diag, via_count):
    source_field = current[0]
    horiz = cond_x[0].astype(jnp.float32)
    vert = cond_y[0].astype(jnp.float32)
    picked = tile_class[0][..., None] == jnp.arange(CLASSES, dtype=jnp.int32)
    lookup = jnp.sum(jnp.where(picked, class_diag, jnp.float32(0.0)), axis=-1)
    diagl = expand(lookup)
    via_g = via_cond * expand(via_count[0].astype(jnp.float32))
    upper = shifted(jnp.stack([vert[-1], diagl[-1]]), "strip", 1)
    vert_up = jnp.concatenate([upper[0:1], vert[:-1]], axis=0)
    diag_up = jnp.concatenate([upper[1:2], diagl[:-1]], axis=0)
    horiz_left = shift_cols(horiz)
    diag_left = shift_cols(diagl)
    diag_upleft = shift_cols(diag_up)
    center = (
        ground_cond
        + horiz
        + horiz_left
        + vert
        + vert_up
        + diagl
        + diag_upleft
        + diag_left
        + diag_up
        + via_g
    )
    rows, cols = source_field.shape
    theta, coeffs = cheby_coeffs(SWEEPS)
    source_local = jnp.sum(source_field * source_field)
    source_total = lax.psum(source_local, "strip")
    voltage = jnp.zeros_like(source_field)
    residual = source_field
    direction = residual / (theta * center)
    sums_list = []
    for step in range(SWEEPS):
        voltage = voltage + direction
        extended = padded_2(direction, (("strip", 0),), 1)
        padded = jnp.pad(extended, ((0, 0), (1, 1)))

        def near(di, dj):
            return padded[1 + di : 1 + di + rows, 1 + dj : 1 + dj + cols]

        beside = horiz * near(0, 1) + horiz_left * near(0, -1)
        beside = beside + vert * near(1, 0) + vert_up * near(-1, 0)
        beside = beside + diagl * near(1, 1) + diag_upleft * near(-1, -1)
        beside = beside + diag_left * near(1, -1) + diag_up * near(-1, 1)
        partner = partner_of(direction)
        residual = residual - (center * direction - beside - via_g * partner)
        local_sum = jnp.sum(residual * residual)
        sums_list.append(lax.psum(local_sum, "strip"))
        if step < SWEEPS - 1:
            keep, push = coeffs[step]
            direction = keep * direction + push * residual / center
    ratios = jnp.sqrt(jnp.stack(sums_list) / source_total)
    return (voltage[None], ratios[:, None])


def solution(mesh):
    placed = (
        P("plane", "strip", None),
        P("plane", "strip", None),
        P("plane", "strip", None),
        P("plane", "strip", None),
        P(),
        P("plane", "strip", None),
    )
    return jax.shard_map(
        on_device,
        mesh=mesh,
        in_specs=placed,
        out_specs=(P("plane", "strip", None), P(None, "plane")),
        check_vma=False,
    )
```

profile of v0, /device:TPU:0, one launch (start us, length us, event | category | flops | bytes accessed | tf_op | source)
XLA Modules:
  0.0 109.6 jit_solution(8972552154183556652)
XLA Ops:
  1.3 0.8 select_reduce_fusion
  2.1 1.0 convert_element_type.27
  3.3 2.5 %collective-permute-start = (f32[2,3072]{1,0:T(2,128)S(1)}, f32[2,3072]{1,0:T(2,128)S(1)}, u32[]{:S(2)}, u32[]{:S(2)}) collective-permute-start(f32[2,3072]{1,0:T(2,128)S(1)} %pad_maximum_fusion.10), channel_id=1, source_target_pairs={{0,1},{1,2},{2,3},{4,5},{5,6},{6,7},{8,9},{9,10},{10,11},{12,13},{... | collective-permute-start | bytes 73736 | tf_op jit(solution)/shard_map/ppermute | solution.py:31
  7.8 0.8 copy-done.2
  8.7 0.7 bitcast_divide_fusion
  9.4 2.4 %collective-permute-start.3 = (f32[64,3072]{1,0:T(8,128)S(1)}, f32[64,3072]{1,0:T(8,128)S(1)}, u32[]{:S(2)}, u32[]{:S(2)}) collective-permute-start(f32[64,3072]{1,0:T(8,128)S(1)} %get-tuple-element.13), channel_id=1, source_target_pairs={{0,4},{4,0},{8,12},{12,8},{16,20},{20,16},{24,28},{28,24},{1,5},{5... | collective-permute-start | bytes 2359304 | tf_op jit(solution)/shard_map/ppermute | solution.py:25
  11.8 3.4 %collective-permute-start.1 = (f32[1,3072]{1,0:T(1,128)S(1)}, f32[1,3072]{1,0:T(1,128)S(1)}, u32[]{:S(2)}, u32[]{:S(2)}) collective-permute-start(f32[1,3072]{1,0:T(1,128)S(1)} %get-tuple-element.24), channel_id=1, source_target_pairs={{0,1},{1,2},{2,3},{4,5},{5,6},{6,7},{8,9},{9,10},{10,11},{12,13},{... | collective-permute-start | bytes 36872 | tf_op jit(solution)/shard_map/ppermute | solution.py:41
  15.2 1.3 %collective-permute-start.2 = (f32[1,3072]{1,0:T(1,128)S(1)}, f32[1,3072]{1,0:T(1,128)S(1)}, u32[]{:S(2)}, u32[]{:S(2)}) collective-permute-start(f32[1,3072]{1,0:T(1,128)S(1)} %get-tuple-element.25), channel_id=1, source_target_pairs={{1,0},{2,1},{3,2},{5,4},{6,5},{7,6},{9,8},{10,9},{11,10},{13,12},{... | collective-permute-start | bytes 36872 | tf_op jit(solution)/shard_map/ppermute | solution.py:42
  16.6 3.1 %collective-permute-done.2 = f32[1,3072]{1,0:T(1,128)S(1)} collective-permute-done((f32[1,3072]{1,0:T(1,128)S(1)}, f32[1,3072]{1,0:T(1,128)S(1)}, u32[]{:S(2)}, u32[]{:S(2)}) %collective-permute-start.2) | collective-permute-done | bytes 12320 | tf_op jit(solution)/shard_map/ppermute | solution.py:42
  20.0 8.9 %collective-permute-done.3 = f32[64,3072]{1,0:T(8,128)S(1)} collective-permute-done((f32[64,3072]{1,0:T(8,128)S(1)}, f32[64,3072]{1,0:T(8,128)S(1)}, u32[]{:S(2)}, u32[]{:S(2)}) %collective-permute-start.3) | collective-permute-done | bytes 786464 | tf_op jit(solution)/shard_map/ppermute | solution.py:25
  28.9 2.2 %multiply_reduce_fusion.2 = (f32[]{:T(128)}, f32[64,3072]{1,0:T(8,128)S(1)}) fusion(f32[64,3072]{1,0:T(8,128)S(1)} %collective-permute-done.3, f32[8,8,24,128]{3,2,1,0:T(8,128)S(1)} %bitcast.88, f32[64,3072]{1,0:T(8,128)S(1)} %pad_maximum_fusion.9, f32[66,3074]{1,0:T(8,128)S(1)} %select_maximum_fusion.6, f32[64,3072]{1,0:T(8,128)S(1)} %bitcast.83, ...), kind=kLoop, calls=%fused_computation.117 | loop fusion | flops 5308415 | bytes 13393924 | tf_op jit(solution)/shard_map/reduce_sum | solution.py:120
  31.4 2.5 %collective-permute-start.6 = (f32[64,3072]{1,0:T(8,128)S(1)}, f32[64,3072]{1,0:T(8,128)S(1)}, u32[]{:S(2)}, u32[]{:S(2)}) collective-permute-start(f32[64,3072]{1,0:T(8,128)S(1)} %divide_add_fusion.2), channel_id=1, source_target_pairs={{0,4},{4,0},{8,12},{12,8},{16,20},{20,16},{24,28},{28,24},{1,5},{5... | collective-permute-start | bytes 2359304 | tf_op jit(solution)/shard_map/ppermute | solution.py:25
  34.0 2.3 %collective-permute-start.4 = (f32[1,3072]{1,0:T(1,128)S(1)}, f32[1,3072]{1,0:T(1,128)S(1)}, u32[]{:S(2)}, u32[]{:S(2)}) collective-permute-start(f32[1,3072]{1,0:T(1,128)S(1)} %get-tuple-element.22), channel_id=1, source_target_pairs={{0,1},{1,2},{2,3},{4,5},{5,6},{6,7},{8,9},{9,10},{10,11},{12,13},{... | collective-permute-start | bytes 36872 | tf_op jit(solution)/shard_map/ppermute | solution.py:41
  36.2 1.3 %collective-permute-start.5 = (f32[1,3072]{1,0:T(1,128)S(1)}, f32[1,3072]{1,0:T(1,128)S(1)}, u32[]{:S(2)}, u32[]{:S(2)}) collective-permute-start(f32[1,3072]{1,0:T(1,128)S(1)} %get-tuple-element.23), channel_id=1, source_target_pairs={{1,0},{2,1},{3,2},{5,4},{6,5},{7,6},{9,8},{10,9},{11,10},{13,12},{... | collective-permute-start | bytes 36872 | tf_op jit(solution)/shard_map/ppermute | solution.py:42
  37.5 2.1 %collective-permute-done.5 = f32[1,3072]{1,0:T(1,128)S(1)} collective-permute-done((f32[1,3072]{1,0:T(1,128)S(1)}, f32[1,3072]{1,0:T(1,128)S(1)}, u32[]{:S(2)}, u32[]{:S(2)}) %collective-permute-start.5) | collective-permute-done | bytes 12320 | tf_op jit(solution)/shard_map/ppermute | solution.py:42
  40.0 12.3 %collective-permute-done.6 = f32[64,3072]{1,0:T(8,128)S(1)} collective-permute-done((f32[64,3072]{1,0:T(8,128)S(1)}, f32[64,3072]{1,0:T(8,128)S(1)}, u32[]{:S(2)}, u32[]{:S(2)}) %collective-permute-start.6) | collective-permute-done | bytes 786464 | tf_op jit(solution)/shard_map/ppermute | solution.py:25
  52.3 2.3 %multiply_reduce_fusion.1 = (f32[]{:T(128)}, f32[64,3072]{1,0:T(8,128)S(1)}) fusion(f32[64,3072]{1,0:T(8,128)S(1)} %get-tuple-element.8, f32[64,3072]{1,0:T(8,128)S(1)} %collective-permute-done.6, f32[8,8,24,128]{3,2,1,0:T(8,128)S(1)} %bitcast.89, f32[64,3072]{1,0:T(8,128)S(1)} %pad_maximum_fusion.9, f32[66,3074]{1,0:T(8,128)S(1)} %select_maximum_fusion.4, ...), kind=kLoop, calls=%fused_computation.116 | loop fusion | flops 5308415 | bytes 13393924 | tf_op jit(solution)/shard_map/reduce_sum | solution.py:120
  54.8 1.8 %collective-permute-start.9 = (f32[64,3072]{1,0:T(8,128)S(1)}, f32[64,3072]{1,0:T(8,128)S(1)}, u32[]{:S(2)}, u32[]{:S(2)}) collective-permute-start(f32[64,3072]{1,0:T(8,128)S(1)} %divide_add_fusion.1), channel_id=1, source_target_pairs={{0,4},{4,0},{8,12},{12,8},{16,20},{20,16},{24,28},{28,24},{1,5},{5... | collective-permute-start | bytes 2359304 | tf_op jit(solution)/shard_map/ppermute | solution.py:25
  56.6 1.4 %collective-permute-start.7 = (f32[1,3072]{1,0:T(1,128)S(1)}, f32[1,3072]{1,0:T(1,128)S(1)}, u32[]{:S(2)}, u32[]{:S(2)}) collective-permute-start(f32[1,3072]{1,0:T(1,128)S(1)} %get-tuple-element.20), channel_id=1, source_target_pairs={{0,1},{1,2},{2,3},{4,5},{5,6},{6,7},{8,9},{9,10},{10,11},{12,13},{... | collective-permute-start | bytes 36872 | tf_op jit(solution)/shard_map/ppermute | solution.py:41
  58.0 1.3 %collective-permute-start.8 = (f32[1,3072]{1,0:T(1,128)S(1)}, f32[1,3072]{1,0:T(1,128)S(1)}, u32[]{:S(2)}, u32[]{:S(2)}) collective-permute-start(f32[1,3072]{1,0:T(1,128)S(1)} %get-tuple-element.21), channel_id=1, source_target_pairs={{1,0},{2,1},{3,2},{5,4},{6,5},{7,6},{9,8},{10,9},{11,10},{13,12},{... | collective-permute-start | bytes 36872 | tf_op jit(solution)/shard_map/ppermute | solution.py:42
  59.3 1.8 %collective-permute-done.8 = f32[1,3072]{1,0:T(1,128)S(1)} collective-permute-done((f32[1,3072]{1,0:T(1,128)S(1)}, f32[1,3072]{1,0:T(1,128)S(1)}, u32[]{:S(2)}, u32[]{:S(2)}) %collective-permute-start.8) | collective-permute-done | bytes 12320 | tf_op jit(solution)/shard_map/ppermute | solution.py:42
  61.4 12.9 %collective-permute-done.9 = f32[64,3072]{1,0:T(8,128)S(1)} collective-permute-done((f32[64,3072]{1,0:T(8,128)S(1)}, f32[64,3072]{1,0:T(8,128)S(1)}, u32[]{:S(2)}, u32[]{:S(2)}) %collective-permute-start.9) | collective-permute-done | bytes 786464 | tf_op jit(solution)/shard_map/ppermute | solution.py:25
  74.3 2.3 %multiply_reduce_fusion = (f32[]{:T(128)}, f32[64,3072]{1,0:T(8,128)S(1)}) fusion(f32[64,3072]{1,0:T(8,128)S(1)} %get-tuple-element.10, f32[64,3072]{1,0:T(8,128)S(1)} %collective-permute-done.9, f32[8,8,24,128]{3,2,1,0:T(8,128)S(1)} %bitcast.90, f32[64,3072]{1,0:T(8,128)S(1)} %pad_maximum_fusion.9, f32[66,3074]{1,0:T(8,128)S(1)} %select_maximum_fusion.2, ...), kind=kLoop, calls=%fused_computation.115 | loop fusion | flops 5308415 | bytes 13393924 | tf_op jit(solution)/shard_map/reduce_sum | solution.py:120
  76.6 2.0 %divide_add_fusion = (f32[64,3072]{1,0:T(8,128)S(1)}, f32[1,64,3072]{2,1,0:T(8,128)}, f32[]{:T(128)}) fusion(f32[64,3072]{1,0:T(8,128)S(1)} %get-tuple-element.14, f32[64,3072]{1,0:T(8,128)S(1)} %get-tuple-element.10, f32[64,3072]{1,0:T(8,128)S(1)} %divide_add_fusion.2, f32[64,3072]{1,0:T(8,128)S(1)} %get-tuple-element.12, f32[1,64,3072]{2,1,0:T(8,128)S(1)} %copy-done.2), kind=kLoop, calls=%fused_computation.119 | loop fusion | flops 2949119 | bytes 5505028 | tf_op jit(solution)/shard_map/add | solution.py:124
  78.6 1.5 %collective-permute-start.12 = (f32[64,3072]{1,0:T(8,128)S(1)}, f32[64,3072]{1,0:T(8,128)S(1)}, u32[]{:S(2)}, u32[]{:S(2)}) collective-permute-start(f32[64,3072]{1,0:T(8,128)S(1)} %get-tuple-element.15), channel_id=1, source_target_pairs={{0,4},{4,0},{8,12},{12,8},{16,20},{20,16},{24,28},{28,24},{1,5},{5... | collective-permute-start | bytes 2359304 | tf_op jit(solution)/shard_map/ppermute | solution.py:25
  80.1 1.3 %collective-permute-start.10 = (f32[1,3072]{1,0:T(1,128)S(1)}, f32[1,3072]{1,0:T(1,128)S(1)}, u32[]{:S(2)}, u32[]{:S(2)}) collective-permute-start(f32[1,3072]{1,0:T(1,128)S(1)} %get-tuple-element.18), channel_id=1, source_target_pairs={{0,1},{1,2},{2,3},{4,5},{5,6},{6,7},{8,9},{9,10},{10,11},{12,13},{... | collective-permute-start | bytes 36872 | tf_op jit(solution)/shard_map/ppermute | solution.py:41
  81.3 1.3 %collective-permute-start.11 = (f32[1,3072]{1,0:T(1,128)S(1)}, f32[1,3072]{1,0:T(1,128)S(1)}, u32[]{:S(2)}, u32[]{:S(2)}) collective-permute-start(f32[1,3072]{1,0:T(1,128)S(1)} %get-tuple-element.19), channel_id=1, source_target_pairs={{1,0},{2,1},{3,2},{5,4},{6,5},{7,6},{9,8},{10,9},{11,10},{13,12},{... | collective-permute-start | bytes 36872 | tf_op jit(solution)/shard_map/ppermute | solution.py:42
  82.7 1.8 %collective-permute-done.11 = f32[1,3072]{1,0:T(1,128)S(1)} collective-permute-done((f32[1,3072]{1,0:T(1,128)S(1)}, f32[1,3072]{1,0:T(1,128)S(1)}, u32[]{:S(2)}, u32[]{:S(2)}) %collective-permute-start.11) | collective-permute-done | bytes 12320 | tf_op jit(solution)/shard_map/ppermute | solution.py:42
  84.8 12.4 %collective-permute-done.12 = f32[64,3072]{1,0:T(8,128)S(1)} collective-permute-done((f32[64,3072]{1,0:T(8,128)S(1)}, f32[64,3072]{1,0:T(8,128)S(1)}, u32[]{:S(2)}, u32[]{:S(2)}) %collective-permute-start.12) | collective-permute-done | bytes 786464 | tf_op jit(solution)/shard_map/ppermute | solution.py:25
  97.2 2.3 %fusion.60 = f32[]{:T(128)} fusion(f32[64,3072]{1,0:T(8,128)S(1)} %get-tuple-element.12, f32[64,3072]{1,0:T(8,128)S(1)} %collective-permute-done.12, f32[64,3072]{1,0:T(8,128)S(1)} %pad_maximum_fusion.9, f32[66,3074]{1,0:T(8,128)S(1)} %select_maximum_fusion, f32[64,3072]{1,0:T(8,128)S(1)} %bitcast.86, f32[64,3072]{1,0:T(8,128)S(1)} %get-tuple-element.15, ...), kind=kLoop, calls=%fused_computation.123 | loop fusion | flops 5308415 | bytes 12607492 | tf_op jit(solution)/shard_map/reduce_sum | solution.py:120
  99.5 6.4 %all-reduce.7 = (f32[1,1]{0,1:T(1,128)}, f32[1,1]{0,1:T(1,128)}, f32[1,1]{0,1:T(1,128)}, f32[1,1]{0,1:T(1,128)}, f32[]{:T(128)}) all-reduce(f32[1,1]{0,1:T(1,128)} %bitcast.16, f32[1,1]{0,1:T(1,128)} %bitcast.15, f32[1,1]{0,1:T(1,128)} %bitcast.14, f32[1,1]{0,1:T(1,128)} %bitcast.13, ...), channel_id=1, replica_groups=mesh['plane'=8,'strip'=4] {'strip'}, use_global_device_ids=true, to_apply=%region_8.9 | all-reduce | flops 5 | bytes 40 | tf_op jit(solution)/shard_map/psum | solution.py:121
  105.9 3.7 %fusion.61 = f32[4,1]{0,1:T(1,128)} fusion(f32[1,1]{0,1:T(1,128)} %get-tuple-element.2, f32[1,1]{0,1:T(1,128)} %get-tuple-element.3, f32[1,1]{0,1:T(1,128)} %get-tuple-element.4, f32[1,1]{0,1:T(1,128)} %get-tuple-element.5, f32[]{:T(128)} %get-tuple-element.6), kind=kLoop, calls=%fused_computation.132 | loop fusion | flops 16 | bytes 36 | tf_op jit(solution)/shard_map/sqrt | solution.py:125
  (41 shorter events, 4.8 us)
Async XLA Ops:
  0.6 0.7 copy-start.4
  3.2 2.6 %copy-start.1 = (bf16[1,64,3072]{2,1,0:T(8,128)(2,1)S(1)}, bf16[1,64,3072]{2,1,0:T(8,128)(2,1)}, u32[]{:S(2)}) copy-start(bf16[1,64,3072]{2,1,0:T(8,128)(2,1)} %param.7) | copy-start | bytes 1179652
  3.3 4.2 %collective-permute-start = (f32[2,3072]{1,0:T(2,128)S(1)}, f32[2,3072]{1,0:T(2,128)S(1)}, u32[]{:S(2)}, u32[]{:S(2)}) collective-permute-start(f32[2,3072]{1,0:T(2,128)S(1)} %pad_maximum_fusion.10), channel_id=1, source_target_pairs={{0,1},{1,2},{2,3},{4,5},{5,6},{6,7},{8,9},{9,10},{10,11},{12,13},{... | collective-permute-start | bytes 73736 | tf_op jit(solution)/shard_map/ppermute | solution.py:31
  5.8 0.7 copy-start.3
  7.4 1.1 %copy-start.2 = (f32[1,64,3072]{2,1,0:T(8,128)S(1)}, f32[1,64,3072]{2,1,0:T(8,128)}, u32[]{:S(2)}) copy-start(f32[1,64,3072]{2,1,0:T(8,128)} %param.6) | copy-start | bytes 2359300
  7.5 1.2 %copy-start = (bf16[1,64,3072]{2,1,0:T(8,128)(2,1)S(1)}, bf16[1,64,3072]{2,1,0:T(8,128)(2,1)}, u32[]{:S(2)}) copy-start(bf16[1,64,3072]{2,1,0:T(8,128)(2,1)} %param.8) | copy-start | bytes 1179652
  9.4 19.5 %collective-permute-start.3 = (f32[64,3072]{1,0:T(8,128)S(1)}, f32[64,3072]{1,0:T(8,128)S(1)}, u32[]{:S(2)}, u32[]{:S(2)}) collective-permute-start(f32[64,3072]{1,0:T(8,128)S(1)} %get-tuple-element.13), channel_id=1, source_target_pairs={{0,4},{4,0},{8,12},{12,8},{16,20},{20,16},{24,28},{28,24},{1,5},{5... | collective-permute-start | bytes 2359304 | tf_op jit(solution)/shard_map/ppermute | solution.py:25
  11.8 4.7 %collective-permute-start.1 = (f32[1,3072]{1,0:T(1,128)S(1)}, f32[1,3072]{1,0:T(1,128)S(1)}, u32[]{:S(2)}, u32[]{:S(2)}) collective-permute-start(f32[1,3072]{1,0:T(1,128)S(1)} %get-tuple-element.24), channel_id=1, source_target_pairs={{0,1},{1,2},{2,3},{4,5},{5,6},{6,7},{8,9},{9,10},{10,11},{12,13},{... | collective-permute-start | bytes 36872 | tf_op jit(solution)/shard_map/ppermute | solution.py:41
  15.2 4.4 %collective-permute-start.2 = (f32[1,3072]{1,0:T(1,128)S(1)}, f32[1,3072]{1,0:T(1,128)S(1)}, u32[]{:S(2)}, u32[]{:S(2)}) collective-permute-start(f32[1,3072]{1,0:T(1,128)S(1)} %get-tuple-element.25), channel_id=1, source_target_pairs={{1,0},{2,1},{3,2},{5,4},{6,5},{7,6},{9,8},{10,9},{11,10},{13,12},{... | collective-permute-start | bytes 36872 | tf_op jit(solution)/shard_map/ppermute | solution.py:42
  31.4 20.9 %collective-permute-start.6 = (f32[64,3072]{1,0:T(8,128)S(1)}, f32[64,3072]{1,0:T(8,128)S(1)}, u32[]{:S(2)}, u32[]{:S(2)}) collective-permute-start(f32[64,3072]{1,0:T(8,128)S(1)} %divide_add_fusion.2), channel_id=1, source_target_pairs={{0,4},{4,0},{8,12},{12,8},{16,20},{20,16},{24,28},{28,24},{1,5},{5... | collective-permute-start | bytes 2359304 | tf_op jit(solution)/shard_map/ppermute | solution.py:25
  34.0 3.6 %collective-permute-start.4 = (f32[1,3072]{1,0:T(1,128)S(1)}, f32[1,3072]{1,0:T(1,128)S(1)}, u32[]{:S(2)}, u32[]{:S(2)}) collective-permute-start(f32[1,3072]{1,0:T(1,128)S(1)} %get-tuple-element.22), channel_id=1, source_target_pairs={{0,1},{1,2},{2,3},{4,5},{5,6},{6,7},{8,9},{9,10},{10,11},{12,13},{... | collective-permute-start | bytes 36872 | tf_op jit(solution)/shard_map/ppermute | solution.py:41
  36.2 3.4 %collective-permute-start.5 = (f32[1,3072]{1,0:T(1,128)S(1)}, f32[1,3072]{1,0:T(1,128)S(1)}, u32[]{:S(2)}, u32[]{:S(2)}) collective-permute-start(f32[1,3072]{1,0:T(1,128)S(1)} %get-tuple-element.23), channel_id=1, source_target_pairs={{1,0},{2,1},{3,2},{5,4},{6,5},{7,6},{9,8},{10,9},{11,10},{13,12},{... | collective-permute-start | bytes 36872 | tf_op jit(solution)/shard_map/ppermute | solution.py:42
  54.8 19.6 %collective-permute-start.9 = (f32[64,3072]{1,0:T(8,128)S(1)}, f32[64,3072]{1,0:T(8,128)S(1)}, u32[]{:S(2)}, u32[]{:S(2)}) collective-permute-start(f32[64,3072]{1,0:T(8,128)S(1)} %divide_add_fusion.1), channel_id=1, source_target_pairs={{0,4},{4,0},{8,12},{12,8},{16,20},{20,16},{24,28},{28,24},{1,5},{5... | collective-permute-start | bytes 2359304 | tf_op jit(solution)/shard_map/ppermute | solution.py:25
  56.6 2.7 %collective-permute-start.7 = (f32[1,3072]{1,0:T(1,128)S(1)}, f32[1,3072]{1,0:T(1,128)S(1)}, u32[]{:S(2)}, u32[]{:S(2)}) collective-permute-start(f32[1,3072]{1,0:T(1,128)S(1)} %get-tuple-element.20), channel_id=1, source_target_pairs={{0,1},{1,2},{2,3},{4,5},{5,6},{6,7},{8,9},{9,10},{10,11},{12,13},{... | collective-permute-start | bytes 36872 | tf_op jit(solution)/shard_map/ppermute | solution.py:41
  58.0 3.1 %collective-permute-start.8 = (f32[1,3072]{1,0:T(1,128)S(1)}, f32[1,3072]{1,0:T(1,128)S(1)}, u32[]{:S(2)}, u32[]{:S(2)}) collective-permute-start(f32[1,3072]{1,0:T(1,128)S(1)} %get-tuple-element.21), channel_id=1, source_target_pairs={{1,0},{2,1},{3,2},{5,4},{6,5},{7,6},{9,8},{10,9},{11,10},{13,12},{... | collective-permute-start | bytes 36872 | tf_op jit(solution)/shard_map/ppermute | solution.py:42
  78.6 18.7 %collective-permute-start.12 = (f32[64,3072]{1,0:T(8,128)S(1)}, f32[64,3072]{1,0:T(8,128)S(1)}, u32[]{:S(2)}, u32[]{:S(2)}) collective-permute-start(f32[64,3072]{1,0:T(8,128)S(1)} %get-tuple-element.15), channel_id=1, source_target_pairs={{0,4},{4,0},{8,12},{12,8},{16,20},{20,16},{24,28},{28,24},{1,5},{5... | collective-permute-start | bytes 2359304 | tf_op jit(solution)/shard_map/ppermute | solution.py:25
  80.1 2.6 %collective-permute-start.10 = (f32[1,3072]{1,0:T(1,128)S(1)}, f32[1,3072]{1,0:T(1,128)S(1)}, u32[]{:S(2)}, u32[]{:S(2)}) collective-permute-start(f32[1,3072]{1,0:T(1,128)S(1)} %get-tuple-element.18), channel_id=1, source_target_pairs={{0,1},{1,2},{2,3},{4,5},{5,6},{6,7},{8,9},{9,10},{10,11},{12,13},{... | collective-permute-start | bytes 36872 | tf_op jit(solution)/shard_map/ppermute | solution.py:41
  81.3 3.1 %collective-permute-start.11 = (f32[1,3072]{1,0:T(1,128)S(1)}, f32[1,3072]{1,0:T(1,128)S(1)}, u32[]{:S(2)}, u32[]{:S(2)}) collective-permute-start(f32[1,3072]{1,0:T(1,128)S(1)} %get-tuple-element.19), channel_id=1, source_target_pairs={{1,0},{2,1},{3,2},{5,4},{6,5},{7,6},{9,8},{10,9},{11,10},{13,12},{... | collective-permute-start | bytes 36872 | tf_op jit(solution)/shard_map/ppermute | solution.py:42
where the time goes:
time: 110 us
  waiting for transfers between devices  55.2 us (50%)
  starting transfers between devices  24.2 us (22%)
  other arithmetic  19.2 us (17%)
  blocking collectives  6.44 us (6%)
  local copies, waits for them, and re-layouts  3.53 us (3%)
    ppermute x4, waiting for transfers between devices, swapped(): return lax.ppermute(block, axis, route)  46.5 us
    reduce_sum x4, other arithmetic, on_device(): local_sum = jnp.sum(residual * residual)  9.01 us
    ppermute x4, waiting for transfers between devices, padded_2(): after = lax.ppermute(initial, axis, down)  8.71 us
    ppermute x4, starting transfers between devices, padded_2(): before = lax.ppermute(last, axis, up)  8.36 us
    ppermute x4, starting transfers between devices, swapped(): return lax.ppermute(block, axis, route)  8.2 us
    psum x1, blocking collectives, on_device(): sums_list.append(lax.psum(local_sum, 'strip'))  6.44 us
    ppermute x4, starting transfers between devices, padded_2(): after = lax.ppermute(initial, axis, down)  5.17 us
    sqrt x1, other arithmetic, on_device(): ratios = jnp.sqrt(jnp.stack(sums_list) / source_total)  3.67 us
  transfers between devices with their start and end apart: 13, of which 8 were waited for; matrix products, arithmetic and copies ran while one was open for 2% of the time, Pallas kernels for 0%

commit v1 on v0

v1 whole, which is shorter than its diff:
```python
import functools

import jax
import jax.numpy as jnp
from jax import lax
from jax.experimental import pallas as pl
from jax.experimental.pallas import tpu as pltpu
from jax.sharding import PartitionSpec as P

TILE_ROWS = 16
TILE_COLS = 128
SWEEPS = 4
VIA_TILES = 24
CHUNKS = 3
WIDE = 3

ground_cond = 0.5
via_cond = 3.0
bound_low = 0.05
bound_high = 2.0

MESH = pl.DeviceIdType.MESH


def cheby_coeffs(sweeps):
    theta = (bound_high + bound_low) / 2.0
    delta = (bound_high - bound_low) / 2.0
    sigma = theta / delta
    rho = 1.0 / sigma
    coeffs = []
    for step in range(sweeps - 1):
        rho_new = 1.0 / (2.0 * sigma - rho)
        coeffs.append((rho_new * rho, 2.0 * rho_new / delta))
        rho = rho_new
    return (theta, coeffs)


def kernel(
    n_strip,
    cur_hbm, cx_hbm, cy_hbm, cls, cdiag, via,
    volt_hbm, ratio_ref,
    cur, cx, cy, volt, dbuf, gxf, gyf, gdrow, cen, inv, w, res,
    send, recv0, recv1, recv2, recv3, hs, hr, cs, cr, sums, sums_in,
    nxt, idx, pos,
    load_sem, out_sem, ps_sem, pr_sem, hs_sem, hr_sem, cs_sem, cr_sem, ss_sem, sr_sem,
):
    recv = (recv0, recv1, recv2, recv3)
    rows, cols = cur.shape
    tr, tc = rows // TILE_ROWS, cols // TILE_COLS
    tiles = tr * tc
    slots = VIA_TILES // CHUNKS
    theta, coeffs = cheby_coeffs(SWEEPS)
    my_plane = lax.axis_index("plane")
    me = lax.axis_index("strip")
    partner = my_plane + 1 - 2 * (my_plane % 2)
    has_up = me > 0
    has_down = me < n_strip - 1

    loads = [
        pltpu.make_async_copy(cy_hbm, cy, load_sem.at[0]),
        pltpu.make_async_copy(cx_hbm, cx, load_sem.at[1]),
        pltpu.make_async_copy(cur_hbm, cur, load_sem.at[2]),
    ]
    for copy in loads:
        copy.start()

    barrier = pltpu.get_barrier_semaphore()
    pl.semaphore_signal(barrier, inc=1, device_id={"plane": partner}, device_id_type=MESH)
    for off in range(1, n_strip):
        pl.semaphore_signal(
            barrier, inc=1, device_id={"strip": (me + off) % n_strip}, device_id_type=MESH
        )

    lane = lax.broadcasted_iota(jnp.int32, (TILE_ROWS, TILE_COLS), 1)
    row_id = lax.broadcasted_iota(jnp.int32, (TILE_ROWS, TILE_COLS), 0)
    first_lane, last_lane, first_row = lane == 0, lane == TILE_COLS - 1, row_id == 0

    def lanes(c):
        if isinstance(c, int):
            return pl.ds(c * TILE_COLS, TILE_COLS)
        return pl.ds(pl.multiple_of(c * TILE_COLS, TILE_COLS), TILE_COLS)

    for k in range(SWEEPS):
        dbuf[k, 0:8, :] = jnp.zeros((8, cols + TILE_COLS), jnp.float32)
        dbuf[k, rows + 8 : rows + 16, :] = jnp.zeros((8, cols + TILE_COLS), jnp.float32)
        dbuf[k, 8 : rows + 8, cols : cols + TILE_COLS] = jnp.zeros((rows, TILE_COLS), jnp.float32)
    gdrow[...] = jnp.zeros_like(gdrow)
    gyf[0:8, :] = jnp.zeros((8, cols), jnp.float32)

    for r in range(tr):
        def fill(c, _, r=r):
            g = cdiag[cls[r, c]]
            gdrow[r + 1 : r + 2, lanes(c)] = jnp.full((1, TILE_COLS), g, jnp.float32)
            return 0
        lax.fori_loop(0, tc, fill, 0)

    loads[0].wait()
    cs[0] = cy[rows - TILE_ROWS : rows, :].astype(jnp.float32)[TILE_ROWS - 1 : TILE_ROWS, :]
    cs[1] = gdrow[tr : tr + 1, :]
    pl.semaphore_wait(barrier, n_strip)

    cond_copy = pltpu.make_async_remote_copy(
        src_ref=cs, dst_ref=cr, send_sem=cs_sem, recv_sem=cr_sem,
        device_id={"strip": (me + 1) % n_strip}, device_id_type=MESH,
    )

    @pl.when(has_down)
    def _():
        cond_copy.start()

    nxt[tiles] = 0
    for r in reversed(range(tr)):
        def back(i, follow, r=r):
            c = tc - 1 - i
            t = r * tc + c
            here = jnp.where(via[r, c] > 0, t, follow)
            nxt[t] = here
            return here
        follow = lax.fori_loop(0, tc, back, jnp.int32(0) if r == tr - 1 else follow)
    count = jnp.int32(0)
    for r in range(tr):
        def forth(c, count, r=r):
            pos[r * tc + c] = jnp.minimum(count, VIA_TILES - 1)
            return count + jnp.where(via[r, c] > 0, 1, 0)
        count = lax.fori_loop(0, tc, forth, count)

    def chain(s, t):
        here = nxt[t]
        idx[s] = here
        return here + 1
    lax.fori_loop(0, VIA_TILES, chain, jnp.int32(0))

    loads[1].wait()

    def convert(c, _):
        gxf[:, lanes(c)] = cx[:, lanes(c)].astype(jnp.float32)
        gyf[8 : rows + 8, lanes(c)] = cy[:, lanes(c)].astype(jnp.float32)
        return 0
    lax.fori_loop(0, tc, convert, 0)
    loads[2].wait()

    def coupling(r, c):
        g = gdrow[r + 1 : r + 2, lanes(c)]
        up = gdrow[r : r + 1, lanes(c)]
        g = jnp.broadcast_to(g, (TILE_ROWS, TILE_COLS))
        return g, jnp.where(first_row, jnp.broadcast_to(up, (TILE_ROWS, TILE_COLS)), g)

    zero = jnp.zeros((TILE_ROWS, TILE_COLS), jnp.float32)

    def prepare(row_tiles, acc):
        def body(i, carry):
            acc, before = carry[0], list(carry[1:])
            for j in range(WIDE):
                c = i * WIDE + j
                for q, r in enumerate(row_tiles):
                    t = r * tc + c
                    own = pl.ds(r * TILE_ROWS, TILE_ROWS)
                    g, g_up = coupling(r, c)
                    side = gxf[own, lanes(c)] + g + g_up
                    left = pltpu.roll(jnp.where(last_lane, before[q], side), 1, 1)
                    before[q] = side
                    gv = via_cond * via[r, c].astype(jnp.float32)
                    center = (
                        (ground_cond + gv) + side + left
                        + gyf[pl.ds(8 + r * TILE_ROWS, TILE_ROWS), lanes(c)]
                        + gyf[pl.ds(7 + r * TILE_ROWS, TILE_ROWS), lanes(c)]
                    )
                    inverse = 1.0 / center
                    source = cur[own, lanes(c)]
                    d0 = source * inverse * (1.0 / theta)
                    cen[t] = center
                    inv[t] = inverse
                    res[t] = source
                    w[t] = d0
                    dbuf[0, pl.ds(8 + r * TILE_ROWS, TILE_ROWS), lanes(c)] = d0
                    acc = acc + source * source
            return (acc, *before)
        return lax.fori_loop(0, tc // WIDE, body, (acc,) + (zero,) * len(row_tiles))[0]

    acc = prepare(tuple(range(1, tr)), zero)

    @pl.when(has_up)
    def _():
        cond_copy.wait_recv()
        gyf[7:8, :] = cr[0]
        gdrow[0:1, :] = cr[1]

    acc = prepare((0,), acc)
    sums[...] = jnp.zeros_like(sums)
    sums[0:1, :] = jnp.sum(acc, axis=0, keepdims=True)

    def part_copy(k, ch):
        part = pl.ds(ch * slots, slots)
        return pltpu.make_async_remote_copy(
            src_ref=send.at[k, part], dst_ref=recv[k].at[part],
            send_sem=ps_sem.at[k, ch], recv_sem=pr_sem.at[k, ch],
            device_id={"plane": partner}, device_id_type=MESH,
        )

    def halo_copy(k, side):
        to = (me + n_strip - 1) % n_strip if side == 0 else (me + 1) % n_strip
        return pltpu.make_async_remote_copy(
            src_ref=hs.at[k, side], dst_ref=hr.at[k, side],
            send_sem=hs_sem.at[k, side], recv_sem=hr_sem.at[k, side],
            device_id={"strip": to}, device_id_type=MESH,
        )

    def send_halos(k):
        hs[k, 0] = dbuf[k, 8:9, 0:cols]
        hs[k, 1] = dbuf[k, rows + 7 : rows + 8, 0:cols]

        @pl.when(has_up)
        def _():
            halo_copy(k, 0).start()

        @pl.when(has_down)
        def _():
            halo_copy(k, 1).start()

    def take_halos(k):
        @pl.when(has_up)
        def _():
            halo_copy(k, 1).wait_recv()
            dbuf[k, 7:8, 0:cols] = hr[k, 1]

        @pl.when(has_down)
        def _():
            halo_copy(k, 0).wait_recv()
            dbuf[k, rows + 8 : rows + 9, 0:cols] = hr[k, 0]

    for ch in range(CHUNKS):
        def pack(s, _):
            send[0, s] = w[idx[s]]
            return 0
        lax.fori_loop(ch * slots, (ch + 1) * slots, pack, 0)
        part_copy(0, ch).start()
    send_halos(0)

    def stencil(k, row_tiles, acc):
        last = k == SWEEPS - 1

        def body(i, carry):
            acc, before = carry[0], list(carry[1:])
            for q, r in enumerate(row_tiles):
                base = 8 + r * TILE_ROWS

                def load(off, c):
                    return dbuf[k, pl.ds(base + off, TILE_ROWS), lanes(c)]

                ahead = [load(off, i * WIDE) for off in (0, -1, 1)]
                for j in range(WIDE):
                    c = i * WIDE + j
                    t = r * tc + c
                    mid, north, south = ahead
                    ahead = [load(off, c + 1) for off in (0, -1, 1)]
                    g, g_up = coupling(r, c)
                    gx = gxf[pl.ds(r * TILE_ROWS, TILE_ROWS), lanes(c)]
                    gy = gyf[pl.ds(base, TILE_ROWS), lanes(c)]
                    gy_up = gyf[pl.ds(base - 1, TILE_ROWS), lanes(c)]
                    cross = g * south + g_up * north
                    cross_ahead = g * ahead[2] + g_up * ahead[1]
                    side = gx * mid + cross
                    east = pltpu.roll(jnp.where(first_lane, ahead[0], mid), TILE_COLS - 1, 1)
                    east_cross = pltpu.roll(
                        jnp.where(first_lane, cross_ahead, cross), TILE_COLS - 1, 1
                    )
                    west = pltpu.roll(jnp.where(last_lane, before[q], side), 1, 1)
                    before[q] = side
                    beside = (gx * east + east_cross) + west + (gy * south + gy_up * north)
                    left = res[t] - cen[t] * mid + beside
                    res[t] = left
                    if last:
                        plain = jnp.where(via[r, c] > 0, 0.0, 1.0)
                        acc = acc + plain * (left * left)
                    else:
                        keep, push = coeffs[k]
                        w[t] = keep * mid + push * (inv[t] * left)
            return (acc, *before)
        return lax.fori_loop(0, tc // WIDE, body, (acc,) + (zero,) * len(row_tiles))[0]

    def merge(k, row_tiles, acc):
        push = coeffs[k][1]

        def body(i, acc):
            for j in range(WIDE):
                c = i * WIDE + j
                for r in row_tiles:
                    t = r * tc + c
                    gv = via_cond * via[r, c].astype(jnp.float32)
                    term = gv * recv[k][pos[t]]
                    left = res[t] + term
                    res[t] = left
                    acc = acc + left * left
                    dbuf[k + 1, pl.ds(8 + r * TILE_ROWS, TILE_ROWS), lanes(c)] = (
                        w[t] + push * (inv[t] * term)
                    )
            return acc
        return lax.fori_loop(0, tc // WIDE, body, acc)

    edge_tiles = (0, tr - 1)
    inner_tiles = tuple(range(1, tr - 1))

    def via_of(t):
        return via[t // tc, t % tc].astype(jnp.float32)

    out_copy = pltpu.make_async_copy(volt, volt_hbm, out_sem)
    for k in range(SWEEPS):
        acc = stencil(k, inner_tiles, zero)
        take_halos(k)
        acc = stencil(k, edge_tiles, acc)
        if k < SWEEPS - 1:
            push = coeffs[k][1]
            for ch in range(CHUNKS):
                part_copy(k, ch).wait_recv()

                def next_slot(s, _):
                    t = idx[s]
                    term = (via_cond * via_of(t)) * recv[k][s]
                    send[k + 1, s] = w[t] + push * (inv[t] * term)
                    return 0
                lax.fori_loop(ch * slots, (ch + 1) * slots, next_slot, 0)
                part_copy(k + 1, ch).start()
            acc = merge(k, edge_tiles, zero)
            send_halos(k + 1)
            acc = merge(k, inner_tiles, acc)
        else:
            def total(c, _):
                own = pl.ds(8, rows)
                volt[:, lanes(c)] = (
                    dbuf[0, own, lanes(c)] + dbuf[1, own, lanes(c)]
                    + dbuf[2, own, lanes(c)] + dbuf[3, own, lanes(c)]
                )
                return 0
            lax.fori_loop(0, tc, total, 0)
            out_copy.start()
            for ch in range(CHUNKS):
                part_copy(k, ch).wait_recv()

                def last_slot(s, acc):
                    t = idx[s]
                    left = res[t] + (via_cond * via_of(t)) * recv[k][s]
                    return acc + left * left
                acc = lax.fori_loop(ch * slots, (ch + 1) * slots, last_slot, acc)
        sums[k + 1 : k + 2, :] = jnp.sum(acc, axis=0, keepdims=True)

    def sum_copy(off):
        return pltpu.make_async_remote_copy(
            src_ref=sums, dst_ref=sums_in.at[off - 1],
            send_sem=ss_sem.at[off - 1], recv_sem=sr_sem.at[off - 1],
            device_id={"strip": (me + off) % n_strip}, device_id_type=MESH,
        )

    for off in range(1, n_strip):
        sum_copy(off).start()

    @pl.when(has_down)
    def _():
        cond_copy.wait_send()
    for k in range(SWEEPS):
        for ch in range(CHUNKS):
            part_copy(k, ch).wait_send()

        @pl.when(has_up)
        def _():
            halo_copy(k, 0).wait_send()

        @pl.when(has_down)
        def _():
            halo_copy(k, 1).wait_send()

    whole = sums[...]
    for off in range(1, n_strip):
        sum_copy(off).wait_recv()
        whole = whole + sums_in[off - 1]
    whole = jnp.sum(whole, axis=1, keepdims=True)
    ratio_ref[...] = jnp.sqrt(whole[1 : SWEEPS + 1, :] / whole[0:1, :])
    for off in range(1, n_strip):
        sum_copy(off).wait_send()
    out_copy.wait()


def solution(mesh):
    n_strip = mesh.shape["strip"]

    def on_device(current, cond_x, cond_y, tile_class, class_diag, via_count):
        rows, cols = current.shape[1:]
        tr, tc = rows // TILE_ROWS, cols // TILE_COLS
        tiles = tr * tc
        f32 = jnp.float32
        tile = (tiles, TILE_ROWS, TILE_COLS)
        packed = (SWEEPS, VIA_TILES, TILE_ROWS, TILE_COLS)
        dma = pltpu.SemaphoreType.DMA
        voltage, ratios = pl.pallas_call(
            functools.partial(kernel, n_strip),
            out_shape=(
                jax.ShapeDtypeStruct((rows, cols), f32),
                jax.ShapeDtypeStruct((SWEEPS, 1), f32),
            ),
            in_specs=[pl.BlockSpec(memory_space=pl.ANY)] * 3
            + [pl.BlockSpec(memory_space=pltpu.SMEM)] * 3,
            out_specs=(
                pl.BlockSpec(memory_space=pl.ANY),
                pl.BlockSpec(memory_space=pltpu.VMEM),
            ),
            scratch_shapes=[
                pltpu.VMEM((rows, cols), f32),
                pltpu.VMEM((rows, cols), jnp.bfloat16),
                pltpu.VMEM((rows, cols), jnp.bfloat16),
                pltpu.VMEM((rows, cols), f32),
                pltpu.VMEM((SWEEPS, rows + 16, cols + TILE_COLS), f32),
                pltpu.VMEM((rows, cols), f32),
                pltpu.VMEM((rows + 8, cols), f32),
                pltpu.VMEM((8, cols), f32),
                pltpu.VMEM(tile, f32),
                pltpu.VMEM(tile, f32),
                pltpu.VMEM(tile, f32),
                pltpu.VMEM(tile, f32),
                pltpu.VMEM(packed, f32),
                pltpu.VMEM(packed[1:], f32),
                pltpu.VMEM(packed[1:], f32),
                pltpu.VMEM(packed[1:], f32),
                pltpu.VMEM(packed[1:], f32),
                pltpu.VMEM((SWEEPS, 2, 1, cols), f32),
                pltpu.VMEM((SWEEPS, 2, 1, cols), f32),
                pltpu.VMEM((2, 1, cols), f32),
                pltpu.VMEM((2, 1, cols), f32),
                pltpu.VMEM((8, TILE_COLS), f32),
                pltpu.VMEM((n_strip - 1, 8, TILE_COLS), f32),
                pltpu.SMEM((tiles + 1,), jnp.int32),
                pltpu.SMEM((VIA_TILES,), jnp.int32),
                pltpu.SMEM((tiles,), jnp.int32),
                dma((3,)),
                dma,
                dma((SWEEPS, CHUNKS)),
                dma((SWEEPS, CHUNKS)),
                dma((SWEEPS, 2)),
                dma((SWEEPS, 2)),
                dma,
                dma,
                dma((n_strip - 1,)),
                dma((n_strip - 1,)),
            ],
            compiler_params=pltpu.CompilerParams(
                collective_id=0, has_side_effects=True, vmem_limit_bytes=48 * 1024 * 1024
            ),
            name="cheby",
        )(current[0], cond_x[0], cond_y[0], tile_class[0], class_diag, via_count[0])
        return (voltage[None], ratios)

    placed = (
        P("plane", "strip", None),
        P("plane", "strip", None),
        P("plane", "strip", None),
        P("plane", "strip", None),
        P(),
        P("plane", "strip", None),
    )
    return jax.shard_map(
        on_device,
        mesh=mesh,
        in_specs=placed,
        out_specs=(P("plane", "strip", None), P(None, "plane")),
        check_vma=False,
    )
```

time: 110 us -> 37.4 us (0.34)
  waiting for transfers between devices: 55.2 us -> 0 us
  Pallas kernels: 0 us -> 31.2 us
  starting transfers between devices: 24.2 us -> 0 us
  other arithmetic: 19.2 us -> 0 us
  blocking collectives: 6.44 us -> 0 us
  local copies, waits for them, and re-layouts: 3.53 us -> 5.28 us
    ppermute x13 -> x0, waiting for transfers between devices: 55.2 us -> none  [the longest x4 46.5 us: swapped(): return lax.ppermute(block, axis, route)]
    pallas_call x0 -> x1, Pallas kernels: none -> 31.2 us  [on_device(): pl.pallas_call(functools.partial(kernel, n_strip), out_shape=(jax.ShapeDt...]
    ppermute x13 -> x0, starting transfers between devices: 24.2 us -> none  [the longest x4 8.36 us: padded_2(): before = lax.ppermute(last, axis, up)]
    reduce_sum x5 -> x0, other arithmetic: 9.78 us -> none  [the longest x4 9.01 us: on_device(): local_sum = jnp.sum(residual * residual)]
    psum x1 -> x0, blocking collectives: 6.44 us -> none  [on_device(): sums_list.append(lax.psum(local_sum, 'strip'))]
    sqrt x1 -> x0, other arithmetic: 3.67 us -> none  [on_device(): ratios = jnp.sqrt(jnp.stack(sums_list) / source_total)]
    unnamed x13 -> x14, local copies, waits for them, and re-layouts: 2.5 us -> 5.28 us
    add x3 -> x0, other arithmetic: 2.45 us -> none  [on_device(): direction = keep * direction + push * residual / center]
  transfers between devices with their start and end apart: 13 -> 0, of which waited for: 8 -> 0; matrix products, arithmetic and copies ran while one was open for 2% -> 0% of each run, Pallas kernels for 0% -> 0%
where the time goes in v1:
time: 37.4 us; the launch traced here: 37.2 us
  Pallas kernels  31.2 us (83%)
  local copies, waits for them, and re-layouts  5.28 us (14%)
  between operations  0.67 us (2%)
    pallas_call x1, Pallas kernels, on_device(): pl.pallas_call(functools.partial(kernel, n_strip), out_shape=(jax.ShapeDt...  31.2 us
    unnamed x14, local copies, waits for them, and re-layouts  5.28 us

profile of v1, /device:TPU:0, one launch (start us, length us, event | category | flops | bytes accessed | tf_op | source)
XLA Modules:
  0.0 37.2 jit_solution(2283473986900223365)
XLA Ops:
  0.6 0.0 copy-start.4
  0.6 0.0 copy-start.3
  0.7 0.0 copy-start.5
  0.7 0.7 %copy-done.4 = s32[1,4,24]{2,1,0:T(4,128)S(1)} copy-done((s32[1,4,24]{2,1,0:T(4,128)S(1)}, s32[1,4,24]{2,1,0:T(4,128)}, u32[]{:S(2)}) %copy-start.4) | copy-done | bytes 408
  1.3 0.0 copy-done.3
  1.3 0.0 copy-done.5
  1.3 0.0 copy-start
  1.3 1.1 %copy-done = f32[1,64,3072]{2,1,0:T(8,128)S(1)} copy-done((f32[1,64,3072]{2,1,0:T(8,128)S(1)}, f32[1,64,3072]{2,1,0:T(8,128)}, u32[]{:S(2)}) %copy-start) | copy-done | bytes 786456
  2.5 0.0 copy-start.1
  2.5 1.0 %copy-done.1 = bf16[1,64,3072]{2,1,0:T(8,128)(2,1)S(1)} copy-done((bf16[1,64,3072]{2,1,0:T(8,128)(2,1)S(1)}, bf16[1,64,3072]{2,1,0:T(8,128)(2,1)}, u32[]{:S(2)}) %copy-start.1) | copy-done | bytes 393240
  3.5 0.0 copy-start.2
  3.5 1.0 %copy-done.2 = bf16[1,64,3072]{2,1,0:T(8,128)(2,1)S(1)} copy-done((bf16[1,64,3072]{2,1,0:T(8,128)(2,1)S(1)}, bf16[1,64,3072]{2,1,0:T(8,128)(2,1)}, u32[]{:S(2)}) %copy-start.2) | copy-done | bytes 393240
  4.5 31.2 %cheby.1 = (f32[64,3072]{1,0:T(8,128)S(1)}, f32[4,1]{1,0:T(4,128)S(1)}) custom-call(f32[64,3072]{1,0:T(8,128)S(1)} %bitcast.6, bf16[64,3072]{1,0:T(8,128)(2,1)S(1)} %bitcast.8, bf16[64,3072]{1,0:T(8,128)(2,1)S(1)} %bitcast.9, s32[4,24]{1,0:T(4,128)S(1)} %bitcast.10, f32[8]{0:T(128)S(1)} %copy-done.5, s32[4,24]{1,0:T(4,128)S(1)} %bitcast.11), custom_call_target="tpu_custom_call" | custom-call | tf_op jit(solution)/shard_map/cheby/pallas_call | solution.py:393
  35.7 0.6 %copy.8 = f32[4,1]{0,1:T(1,128)} copy(f32[4,1]{1,0:T(4,128)S(1)} %get-tuple-element.7) | data formatting | bytes 32
  36.3 0.9 %copy.10 = f32[1,64,3072]{2,1,0:T(8,128)} copy(f32[1,64,3072]{2,1,0:T(8,128)S(1)} %bitcast.7) | data formatting | bytes 1572864
Async XLA Ops:
  0.6 0.7 %copy-start.4 = (s32[1,4,24]{2,1,0:T(4,128)S(1)}, s32[1,4,24]{2,1,0:T(4,128)}, u32[]{:S(2)}) copy-start(s32[1,4,24]{2,1,0:T(4,128)} %param.11) | copy-start | bytes 1156
  0.6 0.7 %copy-start.3 = (s32[1,4,24]{2,1,0:T(4,128)S(1)}, s32[1,4,24]{2,1,0:T(4,128)}, u32[]{:S(2)}) copy-start(s32[1,4,24]{2,1,0:T(4,128)} %param.9) | copy-start | bytes 1156
  0.7 0.7 %copy-start.5 = (f32[8]{0:T(128)S(1)}, f32[8]{0:T(128)}, u32[]{:S(2)}) copy-start(f32[8]{0:T(128)} %cdiag.1) | copy-start | bytes 100
  1.3 1.1 %copy-start = (f32[1,64,3072]{2,1,0:T(8,128)S(1)}, f32[1,64,3072]{2,1,0:T(8,128)}, u32[]{:S(2)}) copy-start(f32[1,64,3072]{2,1,0:T(8,128)} %param.6) | copy-start | bytes 2359300
  2.5 1.0 %copy-start.1 = (bf16[1,64,3072]{2,1,0:T(8,128)(2,1)S(1)}, bf16[1,64,3072]{2,1,0:T(8,128)(2,1)}, u32[]{:S(2)}) copy-start(bf16[1,64,3072]{2,1,0:T(8,128)(2,1)} %param.7) | copy-start | bytes 1179652
  3.5 1.0 %copy-start.2 = (bf16[1,64,3072]{2,1,0:T(8,128)(2,1)S(1)}, bf16[1,64,3072]{2,1,0:T(8,128)(2,1)}, u32[]{:S(2)}) copy-start(bf16[1,64,3072]{2,1,0:T(8,128)(2,1)} %param.8) | copy-start | bytes 1179652

commit v2 on v1

--- a/solution.py
+++ b/solution.py
@@ -41,7 +41,7 @@
     volt_hbm, ratio_ref,
     cur, cx, cy, volt, dbuf, gxf, gyf, gdrow, cen, inv, w, res,
     send, recv0, recv1, recv2, recv3, hs, hr, cs, cr, sums, sums_in,
-    nxt, idx, pos,
+    nxt, idx, pos, via_flat, gvs,
     load_sem, out_sem, ps_sem, pr_sem, hs_sem, hr_sem, cs_sem, cr_sem, ss_sem, sr_sem,
 ):
     recv = (recv0, recv1, recv2, recv3)
@@ -94,20 +94,6 @@
             return 0
         lax.fori_loop(0, tc, fill, 0)
 
-    loads[0].wait()
-    cs[0] = cy[rows - TILE_ROWS : rows, :].astype(jnp.float32)[TILE_ROWS - 1 : TILE_ROWS, :]
-    cs[1] = gdrow[tr : tr + 1, :]
-    pl.semaphore_wait(barrier, n_strip)
-
-    cond_copy = pltpu.make_async_remote_copy(
-        src_ref=cs, dst_ref=cr, send_sem=cs_sem, recv_sem=cr_sem,
-        device_id={"strip": (me + 1) % n_strip}, device_id_type=MESH,
-    )
-
-    @pl.when(has_down)
-    def _():
-        cond_copy.start()
-
     nxt[tiles] = 0
     for r in reversed(range(tr)):
         def back(i, follow, r=r):
@@ -115,6 +101,7 @@
             t = r * tc + c
             here = jnp.where(via[r, c] > 0, t, follow)
             nxt[t] = here
+            via_flat[t] = via[r, c]
             return here
         follow = lax.fori_loop(0, tc, back, jnp.int32(0) if r == tr - 1 else follow)
     count = jnp.int32(0)
@@ -127,9 +114,13 @@
     def chain(s, t):
         here = nxt[t]
         idx[s] = here
+        gvs[s] = via_cond * via_flat[here].astype(jnp.float32)
         return here + 1
     lax.fori_loop(0, VIA_TILES, chain, jnp.int32(0))
 
+    loads[0].wait()
+    cs[0] = cy[rows - TILE_ROWS : rows, :].astype(jnp.float32)[TILE_ROWS - 1 : TILE_ROWS, :]
+    cs[1] = gdrow[tr : tr + 1, :]
     loads[1].wait()
 
     def convert(c, _):
@@ -138,6 +129,16 @@
         return 0
     lax.fori_loop(0, tc, convert, 0)
     loads[2].wait()
+    pl.semaphore_wait(barrier, n_strip)
+
+    cond_copy = pltpu.make_async_remote_copy(
+        src_ref=cs, dst_ref=cr, send_sem=cs_sem, recv_sem=cr_sem,
+        device_id={"strip": (me + 1) % n_strip}, device_id_type=MESH,
+    )
+
+    @pl.when(has_down)
+    def _():
+        cond_copy.start()
 
     def coupling(r, c):
         g = gdrow[r + 1 : r + 2, lanes(c)]
@@ -229,10 +230,8 @@
             dbuf[k, rows + 8 : rows + 9, 0:cols] = hr[k, 0]
 
     for ch in range(CHUNKS):
-        def pack(s, _):
+        for s in range(ch * slots, (ch + 1) * slots):
             send[0, s] = w[idx[s]]
-            return 0
-        lax.fori_loop(ch * slots, (ch + 1) * slots, pack, 0)
         part_copy(0, ch).start()
     send_halos(0)
 
@@ -300,9 +299,6 @@
     edge_tiles = (0, tr - 1)
     inner_tiles = tuple(range(1, tr - 1))
 
-    def via_of(t):
-        return via[t // tc, t % tc].astype(jnp.float32)
-
     out_copy = pltpu.make_async_copy(volt, volt_hbm, out_sem)
     for k in range(SWEEPS):
         acc = stencil(k, inner_tiles, zero)
@@ -312,13 +308,9 @@
             push = coeffs[k][1]
             for ch in range(CHUNKS):
                 part_copy(k, ch).wait_recv()
-
-                def next_slot(s, _):
+                for s in range(ch * slots, (ch + 1) * slots):
                     t = idx[s]
-                    term = (via_cond * via_of(t)) * recv[k][s]
-                    send[k + 1, s] = w[t] + push * (inv[t] * term)
-                    return 0
-                lax.fori_loop(ch * slots, (ch + 1) * slots, next_slot, 0)
+                    send[k + 1, s] = w[t] + (push * gvs[s]) * (inv[t] * recv[k][s])
                 part_copy(k + 1, ch).start()
             acc = merge(k, edge_tiles, zero)
             send_halos(k + 1)
@@ -335,12 +327,9 @@
             out_copy.start()
             for ch in range(CHUNKS):
                 part_copy(k, ch).wait_recv()
-
-                def last_slot(s, acc):
-                    t = idx[s]
-                    left = res[t] + (via_cond * via_of(t)) * recv[k][s]
-                    return acc + left * left
-                acc = lax.fori_loop(ch * slots, (ch + 1) * slots, last_slot, acc)
+                for s in range(ch * slots, (ch + 1) * slots):
+                    left = res[idx[s]] + gvs[s] * recv[k][s]
+                    acc = acc + left * left
         sums[k + 1 : k + 2, :] = jnp.sum(acc, axis=0, keepdims=True)
 
     def sum_copy(off):
@@ -373,7 +362,11 @@
         sum_copy(off).wait_recv()
         whole = whole + sums_in[off - 1]
     whole = jnp.sum(whole, axis=1, keepdims=True)
-    ratio_ref[...] = jnp.sqrt(whole[1 : SWEEPS + 1, :] / whole[0:1, :])
+    at = lax.broadcasted_iota(jnp.int32, (1, SWEEPS), 1)
+    ratios = jnp.zeros((1, SWEEPS), jnp.float32)
+    for k in range(SWEEPS):
+        ratios = jnp.where(at == k, whole[k + 1 : k + 2, :] / whole[0:1, :], ratios)
+    ratio_ref[...] = jnp.sqrt(ratios)
     for off in range(1, n_strip):
         sum_copy(off).wait_send()
     out_copy.wait()
@@ -394,9 +387,9 @@
             functools.partial(kernel, n_strip),
             out_shape=(
                 jax.ShapeDtypeStruct((rows, cols), f32),
-                jax.ShapeDtypeStruct((SWEEPS, 1), f32),
+                jax.ShapeDtypeStruct((1, SWEEPS), f32),
             ),
-            in_specs=[pl.BlockSpec(memory_space=pl.ANY)] * 3
+            in_specs=[pl.BlockSpec(memory_space=pltpu.HBM)] * 3
             + [pl.BlockSpec(memory_space=pltpu.SMEM)] * 3,
             out_specs=(
                 pl.BlockSpec(memory_space=pl.ANY),
@@ -429,6 +422,8 @@
                 pltpu.SMEM((tiles + 1,), jnp.int32),
                 pltpu.SMEM((VIA_TILES,), jnp.int32),
                 pltpu.SMEM((tiles,), jnp.int32),
+                pltpu.SMEM((tiles,), jnp.int32),
+                pltpu.SMEM((VIA_TILES,), f32),
                 dma((3,)),
                 dma,
                 dma((SWEEPS, CHUNKS)),
@@ -441,11 +436,11 @@
                 dma((n_strip - 1,)),
             ],
             compiler_params=pltpu.CompilerParams(
-                collective_id=0, has_side_effects=True, vmem_limit_bytes=48 * 1024 * 1024
+                collective_id=0, has_side_effects=True, vmem_limit_bytes=62 * 1024 * 1024
             ),
             name="cheby",
         )(current[0], cond_x[0], cond_y[0], tile_class[0], class_diag, via_count[0])
-        return (voltage[None], ratios)
+        return (voltage[None], ratios.T)
 
     placed = (
         P("plane", "strip", None),

time: 37.4 us -> 35.1 us (0.939)
  local copies, waits for them, and re-layouts: 5.28 us -> 2.58 us
  Pallas kernels: 31.2 us -> 31.7 us
    unnamed x14 -> x4, local copies, waits for them, and re-layouts: 5.28 us -> 2.58 us
    pallas_call x1, Pallas kernels: 31.2 us -> 31.7 us  [on_device(): pl.pallas_call(functools.partial(kernel, n_strip), out_shape=(jax.ShapeDt...]
where the time goes in v2:
time: 35.1 us; the launch traced here: 34.9 us
  Pallas kernels  31.7 us (90%)
  local copies, waits for them, and re-layouts  2.58 us (7%)
  between operations  0.65 us (2%)
    pallas_call x1, Pallas kernels, on_device(): pl.pallas_call(functools.partial(kernel, n_strip), out_shape=(jax.ShapeDt...  31.7 us
    unnamed x4, local copies, waits for them, and re-layouts  2.58 us

profile of v2, /device:TPU:0, one launch (start us, length us, event | category | flops | bytes accessed | tf_op | source)
XLA Modules:
  0.0 34.9 jit_solution(858192339326691884)
XLA Ops:
  0.6 31.7 %cheby.1 = (f32[64,3072]{1,0:T(8,128)}, f32[1,4]{1,0:T(1,128)}) custom-call(f32[64,3072]{1,0:T(8,128)} %bitcast.7, bf16[64,3072]{1,0:T(8,128)(2,1)} %bitcast.9, bf16[64,3072]{1,0:T(8,128)(2,1)} %bitcast.10, s32[4,24]{1,0:T(4,128)} %bitcast.11, f32[8]{0:T(128)} %cdiag.1, s32[4,24]{1,0:T(4,128)} %bitcast.12), custom_call_target="tpu_custom_call" | custom-call | tf_op jit(solution)/shard_map/cheby/pallas_call | solution.py:386
  32.3 0.0 copy-start
  32.3 2.1 %copy.10 = f32[1,64,3072]{2,1,0:T(8,128)} copy(f32[1,64,3072]{2,1,0:T(8,128)} %bitcast.8) | data formatting | bytes 1572864
  34.4 0.0 copy-done
  34.4 0.5 %copy.11 = f32[4,1]{0,1:T(1,128)} copy(f32[4,1]{0,1:T(1,128)S(1)} %bitcast.13) | data formatting | bytes 32
Async XLA Ops:
  32.3 2.1 %copy-start = (f32[1,4]{1,0:T(1,128)S(1)}, f32[1,4]{1,0:T(1,128)}, u32[]{:S(2)}) copy-start(f32[1,4]{1,0:T(1,128)} %get-tuple-element.5) | copy-start | bytes 52

commit v3 on v2

--- a/solution.py
+++ b/solution.py
@@ -80,10 +80,6 @@
             return pl.ds(c * TILE_COLS, TILE_COLS)
         return pl.ds(pl.multiple_of(c * TILE_COLS, TILE_COLS), TILE_COLS)
 
-    for k in range(SWEEPS):
-        dbuf[k, 0:8, :] = jnp.zeros((8, cols + TILE_COLS), jnp.float32)
-        dbuf[k, rows + 8 : rows + 16, :] = jnp.zeros((8, cols + TILE_COLS), jnp.float32)
-        dbuf[k, 8 : rows + 8, cols : cols + TILE_COLS] = jnp.zeros((rows, TILE_COLS), jnp.float32)
     gdrow[...] = jnp.zeros_like(gdrow)
     gyf[0:8, :] = jnp.zeros((8, cols), jnp.float32)
 
@@ -93,6 +89,20 @@
             gdrow[r + 1 : r + 2, lanes(c)] = jnp.full((1, TILE_COLS), g, jnp.float32)
             return 0
         lax.fori_loop(0, tc, fill, 0)
+
+    loads[0].wait()
+    cs[0] = cy[rows - TILE_ROWS : rows, :].astype(jnp.float32)[TILE_ROWS - 1 : TILE_ROWS, :]
+    cs[1] = gdrow[tr : tr + 1, :]
+    pl.semaphore_wait(barrier, n_strip)
+
+    cond_copy = pltpu.make_async_remote_copy(
+        src_ref=cs, dst_ref=cr, send_sem=cs_sem, recv_sem=cr_sem,
+        device_id={"strip": (me + 1) % n_strip}, device_id_type=MESH,
+    )
+
+    @pl.when(has_down)
+    def _():
+        cond_copy.start()
 
     nxt[tiles] = 0
     for r in reversed(range(tr)):
@@ -104,13 +114,6 @@
             via_flat[t] = via[r, c]
             return here
         follow = lax.fori_loop(0, tc, back, jnp.int32(0) if r == tr - 1 else follow)
-    count = jnp.int32(0)
-    for r in range(tr):
-        def forth(c, count, r=r):
-            pos[r * tc + c] = jnp.minimum(count, VIA_TILES - 1)
-            return count + jnp.where(via[r, c] > 0, 1, 0)
-        count = lax.fori_loop(0, tc, forth, count)
-
     def chain(s, t):
         here = nxt[t]
         idx[s] = here
@@ -118,9 +121,6 @@
         return here + 1
     lax.fori_loop(0, VIA_TILES, chain, jnp.int32(0))
 
-    loads[0].wait()
-    cs[0] = cy[rows - TILE_ROWS : rows, :].astype(jnp.float32)[TILE_ROWS - 1 : TILE_ROWS, :]
-    cs[1] = gdrow[tr : tr + 1, :]
     loads[1].wait()
 
     def convert(c, _):
@@ -129,17 +129,6 @@
         return 0
     lax.fori_loop(0, tc, convert, 0)
     loads[2].wait()
-    pl.semaphore_wait(barrier, n_strip)
-
-    cond_copy = pltpu.make_async_remote_copy(
-        src_ref=cs, dst_ref=cr, send_sem=cs_sem, recv_sem=cr_sem,
-        device_id={"strip": (me + 1) % n_strip}, device_id_type=MESH,
-    )
-
-    @pl.when(has_down)
-    def _():
-        cond_copy.start()
-
     def coupling(r, c):
         g = gdrow[r + 1 : r + 2, lanes(c)]
         up = gdrow[r : r + 1, lanes(c)]
@@ -234,6 +223,19 @@
             send[0, s] = w[idx[s]]
         part_copy(0, ch).start()
     send_halos(0)
+
+    count = jnp.int32(0)
+    for r in range(tr):
+        def forth(c, count, r=r):
+            pos[r * tc + c] = jnp.minimum(count, VIA_TILES - 1)
+            return count + jnp.where(via[r, c] > 0, 1, 0)
+        count = lax.fori_loop(0, tc, forth, count)
+
+
+    for k in range(SWEEPS):
+        dbuf[k, 0:8, :] = jnp.zeros((8, cols + TILE_COLS), jnp.float32)
+        dbuf[k, rows + 8 : rows + 16, :] = jnp.zeros((8, cols + TILE_COLS), jnp.float32)
+        dbuf[k, 8 : rows + 8, cols : cols + TILE_COLS] = jnp.zeros((rows, TILE_COLS), jnp.float32)
 
     def stencil(k, row_tiles, acc):
         last = k == SWEEPS - 1
@@ -436,7 +438,7 @@
                 dma((n_strip - 1,)),
             ],
             compiler_params=pltpu.CompilerParams(
-                collective_id=0, has_side_effects=True, vmem_limit_bytes=62 * 1024 * 1024
+                collective_id=0, has_side_effects=True, vmem_limit_bytes=56 * 1024 * 1024
             ),
             name="cheby",
         )(current[0], cond_x[0], cond_y[0], tile_class[0], class_diag, via_count[0])

time: 35.1 us -> 33.8 us (0.963)
  Pallas kernels: 31.7 us -> 30.4 us
    pallas_call x1, Pallas kernels: 31.7 us -> 30.4 us  [on_device(): pl.pallas_call(functools.partial(kernel, n_strip), out_shape=(jax.ShapeDt...]
where the time goes in v3:
time: 33.8 us; the launch traced here: 33.6 us
  Pallas kernels  30.4 us (90%)
  local copies, waits for them, and re-layouts  2.58 us (8%)
  between operations  0.65 us (2%)
    pallas_call x1, Pallas kernels, on_device(): pl.pallas_call(functools.partial(kernel, n_strip), out_shape=(jax.ShapeDt...  30.4 us
    unnamed x4, local copies, waits for them, and re-layouts  2.58 us

profile of v3, /device:TPU:0, one launch (start us, length us, event | category | flops | bytes accessed | tf_op | source)
XLA Modules:
  0.0 33.6 jit_solution(13110660868357334100)
XLA Ops:
  0.6 30.4 %cheby.1 = (f32[64,3072]{1,0:T(8,128)}, f32[1,4]{1,0:T(1,128)}) custom-call(f32[64,3072]{1,0:T(8,128)} %bitcast.7, bf16[64,3072]{1,0:T(8,128)(2,1)} %bitcast.9, bf16[64,3072]{1,0:T(8,128)(2,1)} %bitcast.10, s32[4,24]{1,0:T(4,128)} %bitcast.11, f32[8]{0:T(128)} %cdiag.1, s32[4,24]{1,0:T(4,128)} %bitcast.12), custom_call_target="tpu_custom_call" | custom-call | tf_op jit(solution)/shard_map/cheby/pallas_call | solution.py:388
  31.0 0.0 copy-start
  31.0 2.1 %copy.10 = f32[1,64,3072]{2,1,0:T(8,128)} copy(f32[1,64,3072]{2,1,0:T(8,128)} %bitcast.8) | data formatting | bytes 1572864
  33.1 0.0 copy-done
  33.1 0.5 %copy.11 = f32[4,1]{0,1:T(1,128)} copy(f32[4,1]{0,1:T(1,128)S(1)} %bitcast.13) | data formatting | bytes 32
Async XLA Ops:
  31.0 2.1 %copy-start = (f32[1,4]{1,0:T(1,128)S(1)}, f32[1,4]{1,0:T(1,128)}, u32[]{:S(2)}) copy-start(f32[1,4]{1,0:T(1,128)} %get-tuple-element.5) | copy-start | bytes 52
